TPU v7x, 256 devices: a whole 4x4x8 slice. The times are simulated.
256 devices in a mesh: tm: 32 (over y, z), space: 8 (over x, core).
Axes of the slice: x: 4, y: 4, z: 8, core: 2. Of those that a mesh axis runs over, the one named last changes fastest.
Arguments:
- frames: bfloat16 [960, 16, 80, 384], P('tm', 'space'), may hold values from -6 to 6
- clip_units: int32 [64], replicated, may hold values from 1 to 11, 288 in all
- out_owner: int32 [512], replicated, may hold values from 0 to 511, as said below
- w_time: bfloat16 [1152, 384], replicated, may hold values from -2 to 2
- norm_gain: float32 [384], replicated, may hold values from 0.1 to 1.9
- w_qk: bfloat16 [384, 768], replicated, may hold values from -64 to 64
- w_value: bfloat16 [384, 384], replicated, may hold values from -0.3125 to 0.3125
- w_proj: bfloat16 [384, 384], replicated, may hold values from -0.3125 to 0.3125
Outputs:
- mixed: bfloat16 [512, 16, 80, 384], P(('tm', 'space'))
Inputs may be any that keep to these rules, and one draw needn't show every extreme that they name: out_owner is a permutation of the 512 slots; out_owner[o] // 16 depends only on o modulo 32.
All inputs are finite; a program needn't handle non-finite values.
Results may differ from a plain program's by a relative error of at most 0.015.
Values may be sent and summed in bfloat16 or wider, within the bound.
No kernel may reach another device: no remote copies, remote signals or barrier semaphores. Data moves between devices by JAX's collectives and lax.ppermute only.
A program may use at most 128 MiB of HBM per device.

v0:
```python
from functools import partial
import math

import jax
import jax.numpy as jnp
from jax import lax
from jax.sharding import PartitionSpec as P


def pick_table(table, index):
    match = index[:, None] == jnp.arange(table.shape[0], dtype=jnp.int32)[None, :]
    return jnp.sum(jnp.where(match, table[None, :], 0), axis=1)


def clip_layout(clip_units, total_out):
    lengths = 4 * clip_units - 3
    starts = jnp.cumsum(lengths) - lengths
    counts = 2 * clip_units - 1
    out_starts = jnp.cumsum(counts) - counts
    order = jnp.arange(total_out, dtype=jnp.int32)
    member = jnp.sum((out_starts[None, :] <= order[:, None]).astype(jnp.int32), axis=1) - 1
    offset = order - pick_table(out_starts, member)
    last_frame = pick_table(starts, member) + 2 * offset
    return (starts, offset, last_frame)


def frame_block(frame, norm_gain, w_qk, w_value, w_proj):
    rows_here, cols_here, channels = frame.shape
    positions = frame.reshape(rows_here * cols_here, channels)
    values32 = positions.astype(jnp.float32)
    inverse_rms = lax.rsqrt(jnp.mean(values32 * values32, axis=1, keepdims=True) + 1e-06)
    normed = (values32 * inverse_rms * norm_gain[None, :]).astype(jnp.bfloat16)
    query_key = jnp.dot(normed, w_qk, preferred_element_type=jnp.float32).astype(jnp.bfloat16)
    queries = query_key[:, :channels]
    key_part = query_key[:, channels:]
    value_rows = jnp.dot(normed, w_value, preferred_element_type=jnp.float32).astype(jnp.bfloat16)
    scores = lax.dot_general(
        queries, key_part, (((1,), (1,)), ((), ())), preferred_element_type=jnp.float32
    )
    scores = scores * (1.0 / math.sqrt(channels))
    shifted = scores - jnp.max(scores, axis=1, keepdims=True)
    powers = jnp.exp(shifted)
    weights = (powers / jnp.sum(powers, axis=1, keepdims=True)).astype(jnp.bfloat16)
    attended = jnp.dot(weights, value_rows, preferred_element_type=jnp.float32).astype(jnp.bfloat16)
    mixed = values32 + jnp.dot(attended, w_proj, preferred_element_type=jnp.float32)
    return mixed.astype(jnp.bfloat16).reshape(frame.shape)


def attend_frames(piece, norm_gain, w_qk, w_value, w_proj):
    worker = partial(frame_block, norm_gain=norm_gain, w_qk=w_qk, w_value=w_value, w_proj=w_proj)
    return lax.map(worker, piece[0])[None]


def transpose_dot(left, right):
    return lax.dot_general(
        left,
        right,
        (((0,), (0,)), ((), ())),
        precision=lax.Precision.HIGHEST,
        preferred_element_type=jnp.float32,
    )


def per_device(frames, clip_units, out_owner, w_time, norm_gain, w_qk, w_value, w_proj):
    n_time = lax.axis_size("tm")
    n_space = lax.axis_size("space")
    fr_dev, rows_dev, columns, channels = frames.shape
    band = rows_dev * columns
    total_out = out_owner.shape[0]
    out_dev = total_out // n_time
    per_peer = (fr_dev + n_time) // n_time
    slot_count = n_time * per_peer
    device = lax.axis_index("tm")
    first_frame = device * fr_dev
    starts, offset, last_frame = clip_layout(clip_units, total_out)
    before = jnp.sum((last_frame < first_frame).astype(jnp.int32))
    far_away = jnp.full((slot_count,), 4 * fr_dev * n_time + 8, jnp.int32)
    no_value = jnp.zeros((slot_count,), jnp.int32)
    window_last = lax.dynamic_slice_in_dim(
        jnp.concatenate([last_frame, far_away]), before, slot_count
    )
    window_offset = lax.dynamic_slice_in_dim(
        jnp.concatenate([offset, no_value]), before, slot_count
    )
    window_owner = lax.dynamic_slice_in_dim(
        jnp.concatenate([out_owner, no_value]), before, slot_count
    )
    step_ids = jnp.arange(slot_count, dtype=jnp.int32)
    exists = before + step_ids < total_out
    dest_slot = window_owner // out_dev * per_peer + step_ids // n_time
    place = window_owner % out_dev
    route = dest_slot[:, None] == step_ids[None, :]
    frame_ids = jnp.arange(fr_dev, dtype=jnp.int32)
    out_ids = jnp.arange(out_dev, dtype=jnp.int32)
    w_side = jnp.concatenate(
        [w_time[:channels], w_time[channels : 2 * channels], w_time[2 * channels :]], axis=1
    )
    terms = jnp.dot(
        frames.reshape(fr_dev * band, channels), w_side, preferred_element_type=jnp.float32
    )
    terms = terms.reshape(fr_dev, band, 3, channels)
    send = jnp.zeros((slot_count, band * channels), jnp.float32)
    valid = jnp.zeros((slot_count,), bool)
    for tap in range(3):
        local_index = window_last - 2 + tap - first_frame
        usable = exists & (local_index >= 0) & (local_index < fr_dev)
        if tap < 2:
            usable = usable & (window_offset >= 1)
        valid = valid | usable
        pick = ((local_index[:, None] == frame_ids[None, :]) & usable[:, None]).astype(jnp.float32)
        select = transpose_dot(route.astype(jnp.float32), pick)
        tap_terms = terms[:, :, tap, :].reshape(fr_dev, band * channels)
        send = send + jnp.dot(
            select, tap_terms, precision=lax.Precision.HIGHEST, preferred_element_type=jnp.float32
        )
    send_place = jnp.sum(jnp.where(route & valid[:, None], (place + 1)[:, None], 0), axis=0) - 1
    received, recv_place = (
        lax.all_to_all(send, "tm", split_axis=0, concat_axis=0, tiled=True),
        lax.all_to_all(send_place, "tm", split_axis=0, concat_axis=0, tiled=True),
    )
    collect = (recv_place[None, :] == out_ids[:, None]).astype(jnp.float32)
    down = jnp.dot(
        collect, received, precision=lax.Precision.HIGHEST, preferred_element_type=jnp.float32
    ).astype(jnp.bfloat16)
    grouped = down.reshape(n_space, out_dev // n_space, rows_dev, columns, channels)
    worker = partial(attend_frames, norm_gain=norm_gain, w_qk=w_qk, w_value=w_value, w_proj=w_proj)
    mixed = worker(lax.all_to_all(grouped, "space", split_axis=0, concat_axis=2, tiled=True))
    return mixed[0]


def solution(mesh):
    placed = (P("tm", "space", None, None), P(), P(), P(), P(), P(), P(), P())
    return jax.shard_map(
        per_device,
        mesh=mesh,
        in_specs=placed,
        out_specs=P(("tm", "space"), None, None, None),
        check_vma=False,
    )
```

profile of v0, /device:TPU:1, one launch (start us, length us, event | category | flops | bytes accessed | tf_op | source)
XLA Modules:
  0.0 490.1 jit_solution(4061952694852239509)
XLA Ops:
  7.8 12.0 %all-to-all-start = ((s32[32,1,1]{2,1,0:T(1,128)}), s32[32,1,1]{2,1,0:T(1,128)S(1)}, u32[]{:S(2)}, u32[]{:S(2)}) async-start(s32[32,1,1]{2,1,0:T(1,128)} %copy.27), calls=%async_computation | async-start | bytes 32768 | tf_op jit(solution)/shard_map/all_to_all | solution.py:119
  21.1 13.3 %convolution_bitcast_fusion = f32[4800,1152]{1,0:T(8,128)} fusion(bf16[4800,384]{1,0:T(8,128)(2,1)} %bitcast.77, bf16[384,384]{1,0:T(8,128)(2,1)S(1)} %get-tuple-element.74, bf16[384,384]{1,0:T(8,128)(2,1)S(1)} %get-tuple-element.75, bf16[384,384]{1,0:T(8,128)(2,1)S(1)} %get-tuple-element.73), kind=kOutput, calls=%fused_computation.18 | convolution fusion | flops 4249387008 | bytes 26689536 | tf_op jit(solution)/shard_map/dot_general | solution.py:98
  34.4 32.1 %reshape.122 = f32[30,160,3,384]{3,2,1,0:T(4,128)} reshape(f32[4800,1152]{1,0:T(8,128)} %convolution_bitcast_fusion) | data formatting | bytes 44236800 | tf_op jit(solution)/shard_map/reshape | solution.py:101
  66.5 89.4 %slice_reduce_fusion = (f32[30,160,384]{2,1,0:T(8,128)}, f32[30,160,384]{2,1,0:T(8,128)}, f32[30,160,384]{2,1,0:T(8,128)}) fusion(f32[30,160,3,384]{3,2,1,0:T(4,128)} %reshape.122), kind=kLoop, calls=%fused_computation.21 | loop fusion | bytes 44236800 | tf_op jit(solution)/shard_map/slice | solution.py:112
  155.9 4.0 pad.6
  159.9 4.6 copy.31
  164.5 4.0 pad.7
  168.5 4.6 copy.32
  173.1 4.0 pad.8
  177.1 8.1 %copy.33 = f32[4,8,160,384]{3,1,2,0:T(8,128)} copy(f32[4,8,160,384]{3,2,1,0:T(8,128)S(1)} %bitcast.69) | data formatting | bytes 15728640
  185.4 7.0 %fusion.43 = f32[32,61440]{1,0:T(8,128)S(1)} fusion(f32[32,30]{1,0:T(8,128)S(1)} %fusion.16, f32[30,61440]{1,0:T(8,128)S(1)} %bitcast.68), kind=kOutput, calls=%fused_computation.93 | convolution fusion | flops 707788800 | bytes 15240960 | tf_op jit(solution)/shard_map/dot_general | solution.py:113
  192.9 9.0 %convolution_add_fusion.2 = f32[32,61440]{1,0:T(8,128)} fusion(f32[32,61440]{1,0:T(8,128)S(1)} %fusion.43, f32[32,30]{1,0:T(8,128)S(1)} %fusion.15, f32[30,61440]{1,0:T(8,128)S(1)} %bitcast.72), kind=kOutput, calls=%fused_computation.16 | convolution fusion | flops 709754880 | bytes 23105280 | tf_op jit(solution)/shard_map/dot_general | solution.py:113
  201.9 9.6 %fusion.6 = f32[32,1,61440]{2,0,1:T(8,128)S(1)} fusion(f32[32,61440]{1,0:T(8,128)} %convolution_add_fusion.2, f32[32,30]{1,0:T(8,128)S(1)} %fusion.14, f32[30,61440]{1,0:T(8,128)S(1)} %bitcast.73), kind=kOutput, calls=%fused_computation.15 | convolution fusion | flops 709754880 | bytes 23105280 | tf_op jit(solution)/shard_map/dot_general | solution.py:113
  211.6 9.3 %copy.28 = f32[32,1,61440]{2,1,0:T(1,128)} copy(f32[32,1,61440]{2,0,1:T(8,128)S(1)} %fusion.6) | data formatting | bytes 15728640 | tf_op jit(solution)/shard_map/all_to_all | solution.py:118
  220.8 9.6 %all-to-all-start.1 = ((f32[32,1,61440]{2,1,0:T(1,128)}), f32[32,1,61440]{2,1,0:T(1,128)}, u32[]{:S(2)}, u32[]{:S(2)}) async-start(f32[32,1,61440]{2,1,0:T(1,128)} %copy.28), calls=%async_computation.1 | async-start | bytes 15728640 | tf_op jit(solution)/shard_map/all_to_all | solution.py:118
  231.1 171.4 %all-to-all-done.1 = f32[32,1,61440]{2,1,0:T(1,128)} async-done(((f32[32,1,61440]{2,1,0:T(1,128)}), f32[32,1,61440]{2,1,0:T(1,128)}, u32[]{:S(2)}, u32[]{:S(2)}) %all-to-all-start.1) | async-done | bytes 7864352 | tf_op jit(solution)/shard_map/all_to_all | solution.py:118
  402.5 10.2 %convolution_convert_fusion.1 = bf16[16,61440]{1,0:T(8,128)(2,1)S(1)} fusion(f32[32,1,61440]{2,1,0:T(1,128)} %all-to-all-done.1, s32[32]{0:T(128)S(1)} %reduce.3), kind=kOutput, calls=%fused_computation.17 | convolution fusion | flops 378470912 | bytes 9830528 | tf_op jit(solution)/shard_map/dot_general | solution.py:122
  414.3 7.9 %all-to-all-start.2 = ((bf16[8,2,2,80,384]{4,3,2,1,0:T(8,128)(2,1)}), bf16[8,2,2,80,384]{4,3,2,1,0:T(8,128)(2,1)S(1)}, u32[]{:S(2)}, u32[]{:S(2)}) async-start(bf16[8,2,2,80,384]{4,3,2,1,0:T(8,128)(2,1)} %bitcast.76), calls=%async_computation.2 | async-start | bytes 3932160 | tf_op jit(solution)/shard_map/all_to_all | solution.py:127
  422.2 24.9 %all-to-all-done.2 = bf16[8,2,2,80,384]{4,3,2,1,0:T(8,128)(2,1)S(1)} async-done(((bf16[8,2,2,80,384]{4,3,2,1,0:T(8,128)(2,1)}), bf16[8,2,2,80,384]{4,3,2,1,0:T(8,128)(2,1)S(1)}, u32[]{:S(2)}, u32[]{:S(2)}) %all-to-all-start.2) | async-done | bytes 1966112 | tf_op jit(solution)/shard_map/all_to_all | solution.py:127
  450.1 39.5 %while.10 = (s32[]{:T(128)}, bf16[2,16,80,384]{3,2,1,0:T(8,128)(2,1)}, bf16[2,16,80,384]{3,2,1,0:T(8,128)(2,1)S(1)}, f32[384]{0:T(512)S(1)}, bf16[384,768]{1,0:T...) while((s32[]{:T(128)}, ...), condition=%wide.region_11.12_spmd, body=%wide.region_7.11_spmd.sunk | while | flops 2776270080 | bytes 28409952 | solution.py:51
  452.1 4.6 convolution_multiply_fusion.2
  458.8 7.6 %online-softmax = f32[1280,384]{1,0:T(8,128)} custom-call(f32[1280,1280]{1,0:T(8,128)} %convolution_multiply_fusion.2, f32[1280,384]{1,0:T(8,128)} %fusion.76), custom_call_target="tpu_custom_call" | custom-call | tf_op online-softmax
  471.8 4.6 convolution_multiply_fusion.2
  478.5 7.6 %online-softmax = f32[1280,384]{1,0:T(8,128)} custom-call(f32[1280,1280]{1,0:T(8,128)} %convolution_multiply_fusion.2, f32[1280,384]{1,0:T(8,128)} %fusion.76), custom_call_target="tpu_custom_call" | custom-call | tf_op online-softmax
  (57 shorter events, 28.1 us)
Async XLA Ops:
  7.8 213.0 %all-to-all-start = ((s32[32,1,1]{2,1,0:T(1,128)}), s32[32,1,1]{2,1,0:T(1,128)S(1)}, u32[]{:S(2)}, u32[]{:S(2)}) async-start(s32[32,1,1]{2,1,0:T(1,128)} %copy.27), calls=%async_computation | async-start | bytes 32768 | tf_op jit(solution)/shard_map/all_to_all | solution.py:119
  192.9 9.0 %copy-start = (f32[4,8,160,384]{3,1,2,0:T(8,128)S(1)}, f32[4,8,160,384]{3,1,2,0:T(8,128)}, u32[]{:S(2)}) copy-start(f32[4,8,160,384]{3,1,2,0:T(8,128)} %copy.33) | copy-start | bytes 23592964
  220.8 181.7 %all-to-all-start.1 = ((f32[32,1,61440]{2,1,0:T(1,128)}), f32[32,1,61440]{2,1,0:T(1,128)}, u32[]{:S(2)}, u32[]{:S(2)}) async-start(f32[32,1,61440]{2,1,0:T(1,128)} %copy.28), calls=%async_computation.1 | async-start | bytes 15728640 | tf_op jit(solution)/shard_map/all_to_all | solution.py:118
  412.7 37.4 %copy-start.2 = (bf16[384,384]{1,0:T(8,128)(2,1)S(1)}, bf16[384,384]{1,0:T(8,128)(2,1)}, u32[]{:S(2)}) copy-start(bf16[384,384]{1,0:T(8,128)(2,1)} %param.16) | copy-start | bytes 884740
  412.7 37.4 %copy-start.3 = (bf16[384,384]{1,0:T(8,128)(2,1)S(1)}, bf16[384,384]{1,0:T(8,128)(2,1)}, u32[]{:S(2)}) copy-start(bf16[384,384]{1,0:T(8,128)(2,1)} %param.17) | copy-start | bytes 884740
  412.7 37.4 %copy-start.4 = (f32[384]{0:T(512)S(1)}, f32[384]{0:T(512)}, u32[]{:S(2)}) copy-start(f32[384]{0:T(512)} %param.14) | copy-start | bytes 4612
  412.8 37.4 %copy-start.5 = (bf16[384,768]{1,0:T(8,128)(2,1)S(1)}, bf16[384,768]{1,0:T(8,128)(2,1)}, u32[]{:S(2)}) copy-start(bf16[384,768]{1,0:T(8,128)(2,1)} %param.15) | copy-start | bytes 1769476
  414.3 32.8 %all-to-all-start.2 = ((bf16[8,2,2,80,384]{4,3,2,1,0:T(8,128)(2,1)}), bf16[8,2,2,80,384]{4,3,2,1,0:T(8,128)(2,1)S(1)}, u32[]{:S(2)}, u32[]{:S(2)}) async-start(bf16[8,2,2,80,384]{4,3,2,1,0:T(8,128)(2,1)} %bitcast.76), calls=%async_computation.2 | async-start | bytes 3932160 | tf_op jit(solution)/shard_map/all_to_all | solution.py:127
  447.1 1.3 copy-start.1
where the time goes:
time: 500 us; the launch traced here: 490 us
  waiting for transfers between devices  196 us (39%)
  local copies, waits for them, and re-layouts  169 us (34%)
  matrix products  70.2 us (14%)
  starting transfers between devices  29.5 us (6%)
  Pallas kernels  15.1 us (3%)
  other arithmetic  7.19 us (1%)
    all_to_all x1, waiting for transfers between devices, per_device(): lax.all_to_all(send, 'tm', split_axis=0, concat_axis=0, tiled=True)  171 us
    slice x1, local copies, waits for them, and re-layouts, per_device(): tap_terms = terms[:, :, tap, :].reshape(fr_dev, band * channels)  89.4 us
    reshape x1, local copies, waits for them, and re-layouts, per_device(): terms = terms.reshape(fr_dev, band, 3, channels)  32.1 us
    unnamed x19, local copies, waits for them, and re-layouts  32.1 us
    dot_general x3, matrix products, per_device(): jnp.dot(select, tap_terms, precision=lax.Precision.HIGHEST, preferred_ele...  25.6 us
    all_to_all x1, waiting for transfers between devices, per_device(): lax.all_to_all(grouped, 'space', split_axis=0, concat_axis=2, tiled=True)  24.9 us
    unnamed x2, Pallas kernels  15.1 us
    dot_general x1, matrix products, per_device(): jnp.dot(frames.reshape(fr_dev * band, channels), w_side, preferred_elemen...  13.3 us
  transfers between devices with their start and end apart: 3, of which 2 were waited for; matrix products, arithmetic and copies ran while one was open for 41% of the time, Pallas kernels for 0%

commit v1 on v0

v1 whole, which is shorter than its diff:
```python
from functools import partial
import math

import jax
import jax.numpy as jnp
from jax import lax
from jax.experimental import pallas as pl
from jax.experimental.pallas import tpu as pltpu
from jax.sharding import PartitionSpec as P

SHARES = (5, 5)
GROUP = 9
COPIES = 5
NY, NZ = 4, 8
SWAP = 13
MERGED = (8, 6, 6, 6)
YCAP = 5
MIB = 1024 * 1024


def conv_kernel(slots_row, first, plan_ref, frames_ref, halo_ref, w_ref, *refs):
    *out_refs, weights, held, lhs, sems = refs
    rows, channels = held.shape[-2:]
    band = pl.ds(first, rows)
    halo, frames = halo_ref.shape[0], frames_ref.shape[0]
    per_copy = frames // COPIES
    copies = [
        pltpu.make_async_copy(
            frames_ref.at[pl.ds(i * per_copy, per_copy), band],
            held.at[pl.ds(halo + i * per_copy, per_copy)],
            sems.at[i],
        )
        for i in range(COPIES)
    ]
    copies.append(pltpu.make_async_copy(halo_ref.at[:, band], held.at[pl.ds(0, halo)], sems.at[COPIES]))
    copies.append(pltpu.make_async_copy(w_ref, weights, sems.at[COPIES + 1]))
    for copy in copies:
        copy.start()
    for copy in copies:
        copy.wait()
    count = plan_ref[ROWS_OF["own"], 0]

    def one_group(group, carry):
        for k in range(GROUP):
            slot = jnp.minimum(group * GROUP + k, count - 1)
            last = plan_ref[ROWS_OF["last"], slot]
            early = plan_ref[ROWS_OF["early"], slot] == 1
            here = pl.ds(k * rows, rows)
            lhs[here, 2 * channels :] = held[last + 2]
            for tap in range(2):
                there = pl.ds(tap * channels, channels)

                @pl.when(early)
                def _():
                    lhs[here, there] = held[last + tap]

                @pl.when(jnp.logical_not(early))
                def _():
                    lhs[here, there] = jnp.zeros((rows, channels), lhs.dtype)
        down = jnp.dot(lhs[...], weights[...], preferred_element_type=jnp.float32)
        for k in range(GROUP):
            slot = jnp.minimum(group * GROUP + k, count - 1)
            target, begin = plan_ref[slots_row, slot], 0
            piece = down[k * rows : (k + 1) * rows].astype(held.dtype)
            for out_ref in out_refs:
                slots = out_ref.shape[0]

                @pl.when((target >= begin) & (target < begin + slots))
                def _():
                    out_ref[jnp.clip(target - begin, 0, slots - 1)] = piece

                begin += slots
        return carry

    lax.fori_loop(0, lax.div(count + GROUP - 1, GROUP), one_group, 0)


def conv(plan, slots_row, frames, halo, w_time, first, rows, outs):
    count, band, channels = frames.shape
    return pl.pallas_call(
        partial(conv_kernel, slots_row, first),
        grid=(1,),
        out_shape=[jax.ShapeDtypeStruct((slots, rows, channels), frames.dtype) for slots in outs],
        in_specs=[
            pl.BlockSpec(memory_space=pltpu.SMEM),
            pl.BlockSpec(memory_space=pltpu.HBM),
            pl.BlockSpec(memory_space=pltpu.HBM),
            pl.BlockSpec(memory_space=pltpu.HBM),
        ],
        out_specs=[pl.BlockSpec((slots, rows, channels), lambda i: (0, 0, 0)) for slots in outs],
        scratch_shapes=[
            pltpu.VMEM(w_time.shape, w_time.dtype),
            pltpu.VMEM((count + 2, rows, channels), frames.dtype),
            pltpu.VMEM((GROUP * rows, 3 * channels), frames.dtype),
            pltpu.SemaphoreType.DMA((COPIES + 2,)),
        ],
        compiler_params=pltpu.CompilerParams(vmem_limit_bytes=24 * MIB),
        cost_estimate=pl.CostEstimate(
            flops=count * rows * 3 * channels * channels,
            bytes_accessed=4 * (count + sum(outs)) * rows * channels,
            transcendentals=0,
        ),
        name="temporal_conv",
    )(plan, frames, halo, w_time)


def place_kernel(row, sizes, outs, plan_ref, *refs):
    out_refs = refs[len(refs) - len(outs) :]
    at = 0
    for ref, size in zip(refs, sizes):

        def one_slot(j, carry, ref=ref, at=at):
            slot = plan_ref[row, at + j]
            begin = 0
            for out_ref, slots in zip(out_refs, outs):

                @pl.when((slot >= begin) & (slot < begin + slots))
                def _():
                    out_ref[jnp.clip(slot - begin, 0, slots - 1)] = ref[j]

                begin += slots
            return carry

        lax.fori_loop(0, size, one_slot, 0, unroll=True)
        at += size


def place(plan, row, outs, *sources, after=()):
    rows, channels = sources[0][0].shape[1:]
    sizes = [size for _, size in sources]
    results = pl.pallas_call(
        partial(place_kernel, row, sizes, outs),
        grid=(1,),
        out_shape=[jax.ShapeDtypeStruct((slots, rows, channels), sources[0][0].dtype) for slots in outs],
        in_specs=[pl.BlockSpec(memory_space=pltpu.SMEM)]
        + [pl.BlockSpec((size, rows, channels), lambda i: (0, 0, 0)) for size in sizes]
        + [pl.BlockSpec(memory_space=pl.ANY)] * len(after),
        out_specs=[pl.BlockSpec((slots, rows, channels), lambda i: (0, 0, 0)) for slots in outs],
        compiler_params=pltpu.CompilerParams(vmem_limit_bytes=16 * MIB),
        cost_estimate=pl.CostEstimate(flops=0, bytes_accessed=sum(outs), transcendentals=0),
        name="place_slots",
    )(plan, *[array for array, _ in sources], *after)
    return results if len(outs) > 1 else results[0]


ROWS_OF = {"own": 0, "last": 1, "early": 2, "ring": 3, "direct_out": 4, "collect": 5, "direct_in": 6, "merge": 7, "columns": 8, "collect_near": 9}
PLAN_ROWS = 16
LANES = 128


def plan_kernel(fr_dev, n_space, place_ref, units_ref, owner_ref, out_ref):
    n_clips = units_ref.shape[1]
    out_dev, n_time = owner_ref.shape
    bits = n_time.bit_length() - 1
    out_bits = out_dev.bit_length() - 1
    time = place_ref[0]
    y, z = lax.shift_right_logical(time, 3), time & (NZ - 1)
    up = (z + place_ref[1]) & 1
    sign = 2 * up - 1

    def sub(rows, columns):
        return lax.broadcasted_iota(jnp.int32, (rows, columns), 0)

    def lane(rows, columns):
        return lax.broadcasted_iota(jnp.int32, (rows, columns), 1)

    def total(mask, value, axis):
        picked = jnp.where(mask, value, 0).astype(jnp.float32)
        return jnp.sum(picked, axis=axis, keepdims=True).astype(jnp.int32)

    def flip(row):
        n = row.shape[1]
        return total(sub(n, n) == lane(n, n), row, 1)

    units = units_ref[...]
    lengths, counts = 4 * units - 3, 2 * units - 1
    square = (n_clips, n_clips)
    lengths_col, counts_col = flip(lengths), flip(counts)
    starts = total(sub(*square) < lane(*square), lengths_col, 0)
    starts_col = total(lane(*square) < sub(*square), lengths, 1)
    first_col = lax.shift_right_logical(starts_col + sub(n_clips, 1), 1)

    def before(edges):
        return jnp.clip(lax.shift_right_arithmetic(edges - starts + 1, 1), 0, counts)

    low_col = total(True, before(fr_dev * sub(n_time, n_clips)), 1)
    high_col = total(True, before(fr_dev * sub(n_time, n_clips) + fr_dev), 1)
    ts, tl = sub(n_time, n_time), lane(n_time, n_time)
    low = total(ts == tl, low_col, 0)
    high = total(ts == tl, high_col, 0)
    owners = lax.shift_right_logical(owner_ref[0:1, :], out_bits)
    owners_col = flip(owners)
    residue = total(owners_col == tl, ts, 0)
    residue_col = total(owners == ts, tl, 1)

    def put(name, row):
        out_ref[ROWS_OF[name] : ROWS_OF[name] + 1, 0 : row.shape[1]] = row

    def in_window(residues, lows, highs):
        return ((residues - lows) & (n_time - 1)) < highs - lows

    my_low = total(tl[0:1] == time, low, 1)
    my_high = total(tl[0:1] == time, high, 1)
    outs = my_low + tl[0:1]
    first_last = first_col + counts_col
    inside = (first_col <= outs) & (outs < first_last)
    lasts = total(inside, starts_col - 2 * first_col, 0) + 2 * outs - time * fr_dev
    put("last", lasts)
    put("early", total(inside & (outs > first_col), 1, 0))
    dests = total(ts == (outs & (n_time - 1)), owners_col, 0)
    put("direct_out", dests)
    mine = in_window(residue_col, my_low, my_high)

    def apart_of(device):
        return (sign * ((device & (NZ - 1)) - z)) & (NZ - 1)

    def key_of(device):
        return apart_of(device) * NY + lax.shift_right_logical(device, 3)

    far, far_d = apart_of(ts) >= 4, apart_of(dests) >= 4
    lower = mine & (key_of(ts) < key_of(dests)) & ((far & far_d) | (apart_of(ts) == apart_of(dests)))
    put("ring", jnp.where(far_d, 4 * NY, NY * apart_of(dests)) + total(lower, 1, 0))

    spot = lane(1, LANES)
    partner = y * NZ + ((z - sign) & (NZ - 1))
    mate_low = total(tl[0:1] == partner, low, 1)
    mate_high = total(tl[0:1] == partner, high, 1)
    mate = in_window(residue_col, mate_low, mate_high) & (apart_of(ts[:, 0:1]) < 4)
    mate_row = total(ts == tl, mate.astype(jnp.int32), 0)
    mine_row = total(ts == tl, mine.astype(jnp.int32), 0)
    mate_key_s, mate_key_l = (7 - apart_of(ts)) * NY + lax.shift_right_logical(ts, 3), (
        7 - apart_of(tl)
    ) * NY + lax.shift_right_logical(tl, 3)
    sent_at = total(mate_key_l < mate_key_s, mate_row, 1)
    same_column = (ts & (NZ - 1)) == (tl & (NZ - 1))
    merged_at = total(same_column, mine_row, 1) + total(same_column & (tl < ts), mate_row, 1)
    start_of = [sum(MERGED[:i]) for i in range(4)]
    none = sum(MERGED)

    def start_at(apart):
        return jnp.where(apart == 0, start_of[0], start_of[1] + MERGED[1] * (apart - 1))

    merged_at = merged_at + start_at(apart_of(ts[:, 0:1]))
    from_mate = total(mate & (sent_at == lane(n_time, LANES) - 4 * NY), merged_at - none, 0)
    wide = lane(n_time, LANES)
    own_count = total(mine & (apart_of(sub(n_time, LANES)) == lax.shift_right_logical(wide, 2)), 1, 0)
    rank = spot & (NY - 1)
    from_own = jnp.where(rank < own_count, start_at(lax.shift_right_logical(spot, 2)) + rank - none, 0)
    put("merge", none + jnp.where(spot < 4 * NY, from_own, from_mate))

    each = sub(n_time, n_time)
    other = lane(n_time, n_time)

    def parts_of(e):
        return lax.shift_right_logical(e, 2), e & (NY - 1)

    apart, k = parts_of(each)
    apart_o, k_o = parts_of(other)
    e_low = total(tl == y * NZ + ((z + sign * apart) & (NZ - 1)), low, 1)
    e_high = total(tl == y * NZ + ((z + sign * apart) & (NZ - 1)), high, 1)
    e_residue = total(tl == NZ * k + z, residue, 1)
    held = in_window(e_residue, e_low, e_high)
    held_row = total(ts == tl, held.astype(jnp.int32), 0)
    sooner = ((z + sign * apart_o) & (NZ - 1)) < ((z + sign * apart) & (NZ - 1))
    y_rank = total((k_o == k) & sooner, held_row, 1)
    y_slot = ((k[:, 0:1] - y) & (NY - 1)) * YCAP + y_rank
    none = NY * YCAP

    def list_of(a):
        return jnp.where((a == 0) | (a == 7), 0, jnp.where(a <= 2, 1, jnp.where(a <= 4, 3, 2)))

    def order_of(a, k):
        second = (a == 7) | (a == 2) | (a == 5) | (a == 4)
        return jnp.where(second, NY, 0) + k

    which = list_of(apart)
    earlier = (which == list_of(apart_o)) & (order_of(apart_o, k_o) < order_of(apart, k))
    listed = which[:, 0:1]
    listed = jnp.where(listed == 0, 0, MERGED[0] + MERGED[1] * (3 - listed))
    position = listed + total(earlier, held_row, 1)
    hit = held & (position == lane(n_time, LANES))
    put("columns", none + total(hit, y_slot - none, 0))

    my_residue = total(tl[0:1] == time, residue, 1)
    each_dev = out_dev // n_space
    my_outs = my_residue + n_time * sub(out_dev, 1)
    places = total(lane(out_dev, n_time) == my_residue, owner_ref[...], 1) & (out_dev - 1)
    space = place_ref[1]
    to_space = lax.shift_right_logical(places, each_dev.bit_length() - 1)
    ahead = lax.shift_right_logical(to_space, 1) - lax.shift_right_logical(space, 1)
    ahead = ahead & (n_space // 2 - 1)
    crossed = (to_space & 1) ^ (space & 1)
    near = (2 * ahead + crossed) * each_dev + (places & (each_dev - 1))
    y_from = jnp.zeros((out_dev, 1), jnp.int32)
    below = jnp.zeros((out_dev, 1), jnp.int32)
    for number in range(1, NY):
        edge = low[:, NZ * number : NZ * number + 1]
        past = my_outs >= edge
        y_from = y_from + past.astype(jnp.int32)
        under = jnp.maximum(0, lax.shift_right_arithmetic(edge - my_residue + n_time - 1, bits))
        below = jnp.where(past, under, below)
    far_first = (y - y_from) & (NY - 1)
    far_first = jnp.where(far_first == 1, 2, jnp.where(far_first == 2, 1, far_first))
    slot = far_first * YCAP + sub(out_dev, 1) - below
    put("collect", out_dev + total(slot == lane(out_dev, LANES), places - out_dev, 0))
    put("collect_near", out_dev + total(slot == lane(out_dev, LANES), near - out_dev, 0))
    t_from = total(my_outs >= high, 1, 1)
    put("direct_in", out_dev + total(t_from == lane(out_dev, LANES), places - out_dev, 0))

    everywhere = in_window(residue, low_col, high_col).astype(jnp.float32)
    same_ring = lax.shift_right_logical(ts, 3) == lax.shift_right_logical(tl, 3)

    def gathered(mask, right):
        return jnp.dot(mask.astype(jnp.float32), right, preferred_element_type=jnp.float32)

    arriving = gathered(same_ring, everywhere)
    worst = jnp.max(arriving - YCAP, axis=1, keepdims=True)
    alike = (ts & (NZ - 1)) == (tl & (NZ - 1))
    pairs = jnp.dot(everywhere, alike.astype(jnp.float32), preferred_element_type=jnp.float32)
    for way in (1, -1):
        ahead = (way * (tl - ts)) & (NZ - 1)
        behind = (way * (ts - tl)) & (NZ - 1)
        swapped = jnp.sum(jnp.where(ahead >= 4, everywhere, 0.0), axis=1, keepdims=True)
        worst = jnp.maximum(worst, swapped - SWAP)
        sums = gathered(same_ring & (behind < 2), pairs)
        over = jnp.where((ahead >= 1) & (ahead <= 3), sums, 0.0) - MERGED[1]
        worst = jnp.maximum(worst, jnp.max(over, axis=1, keepdims=True))
    worst = jnp.max(worst, axis=0, keepdims=True).astype(jnp.int32)
    put("own", jnp.where(spot == 0, my_high - my_low, worst))


def make_plan(clip_units, out_owner, here, fr_dev, n_space):
    n_time = NY * NZ
    vmem = pl.BlockSpec(memory_space=pltpu.VMEM)
    return pl.pallas_call(
        partial(plan_kernel, fr_dev, n_space),
        out_shape=jax.ShapeDtypeStruct((PLAN_ROWS, LANES), jnp.int32),
        in_specs=[pl.BlockSpec(memory_space=pltpu.SMEM), vmem, vmem],
        out_specs=vmem,
        compiler_params=pltpu.CompilerParams(vmem_limit_bytes=8 * MIB),
        name="routing_plan",
    )(here, clip_units.reshape(1, -1), out_owner.reshape(-1, n_time))


def ring_perm(dy):
    return [
        (a * NZ + b, (a + dy) % NY * NZ + b) for a in range(NY) for b in range(NZ)
    ]


def signed_perm(n_space, apart):
    moves = []
    for time in range(NY * NZ):
        for space in range(n_space):
            z = time % NZ
            sign = 1 if (z + space) % 2 else -1
            to = time - z + (z + sign * apart) % NZ
            moves.append((time * n_space + space, to * n_space + space))
    return moves


def swap_space(placed, n_space):
    each, rows, channels = placed.shape[0] // n_space, *placed.shape[1:]
    placed = placed.reshape(n_space, each, rows, channels)
    return lax.all_to_all(placed, "space", split_axis=0, concat_axis=0, tiled=True)


def far_first(n_space):
    half = n_space // 2
    return sorted(range(n_space), key=lambda o: (o != 0, -min(o // 2, half - o // 2), o))


def to_space(placed, n_space):
    each, half = placed.shape[0] // n_space, n_space // 2
    arrived = [placed]
    for offset in far_first(n_space)[1:]:
        ahead, cross = offset // 2, offset % 2
        moves = [(x * 2 + c, (x + ahead) % half * 2 + (c ^ cross)) for x in range(half) for c in range(2)]
        arrived.append(lax.ppermute(placed[each * offset : each * (offset + 1)], "space", moves))
    return arrived


def by_rings(plan, own, out_dev, n_space):
    both = ("tm", "space")
    chunks = range(len(own))
    swapped = [lax.ppermute(far, both, signed_perm(n_space, -1)) for _, far in own]
    merged = [
        place(
            plan,
            ROWS_OF["merge"],
            MERGED,
            (own[c][0], 4 * NY),
            (swapped[c], SWAP),
        )
        for c in chunks
    ]
    arrived = []
    for c in chunks:
        moved = {
            apart: lax.ppermute(merged[c][apart], both, signed_perm(n_space, apart)) for apart in (3, 2, 1)
        }
        arrived.append([merged[c][0]] + [moved[apart] for apart in (3, 2, 1)])
    columns = []
    for c in chunks:
        sources = zip(arrived[c], MERGED)
        ahead = merged[c + 1][:1] if c + 1 < len(own) else []
        columns.append(place(plan, ROWS_OF["columns"], (YCAP,) * NY, *sources, after=ahead))
    parts = []
    for c in chunks:
        last = c + 1 == len(own)
        moved = [columns[c][0]] + [lax.ppermute(columns[c][dy], "tm", ring_perm(dy)) for dy in (2, 1, 3)]
        table = "collect_near" if last else "collect"
        ahead = [] if last else columns[c + 1][:1]
        placed = place(plan, ROWS_OF[table], (out_dev,), *[(m, YCAP) for m in moved], after=ahead)
        parts.append(placed if last else swap_space(placed, n_space))
    return parts


def per_device(frames, clip_units, out_owner, w_time, norm_gain, w_qk, w_value, w_proj):
    n_time = lax.axis_size("tm")
    n_space = lax.axis_size("space")
    fr_dev, rows_dev, columns, channels = frames.shape
    out_dev = out_owner.shape[0] // n_time
    band = rows_dev * columns
    pieces = band // 16
    edges = [round(pieces * sum(SHARES[:i]) / sum(SHARES)) * 16 for i in range(len(SHARES) + 1)]
    rows_of = list(zip(edges[:-1], [b - a for a, b in zip(edges[:-1], edges[1:])]))
    time = lax.axis_index("tm").astype(jnp.int32)
    frames = frames.reshape(fr_dev, band, channels)
    halo = lax.ppermute(frames[fr_dev - 2 :], "tm", [(i, i + 1) for i in range(n_time - 1)])
    here = jnp.stack([time, lax.axis_index("space").astype(jnp.int32)])
    plan = make_plan(clip_units, out_owner, here, fr_dev, n_space)
    fits = plan[ROWS_OF["own"], 1] <= 0
    def rings():
        own = [conv(plan, ROWS_OF["ring"], frames, halo, w_time, *r, (4 * NY, SWAP)) for r in rows_of]
        return by_rings(plan, own, out_dev, n_space)

    def direct():
        send = conv(plan, ROWS_OF["direct_out"], frames, halo, w_time, 0, band, (n_time,))[0]
        received = lax.all_to_all(send, "tm", split_axis=0, concat_axis=0, tiled=True)
        placed = place(plan, ROWS_OF["direct_in"], (out_dev,), (received, n_time))
        parts = [swap_space(placed[:, first : first + rows], n_space) for first, rows in rows_of[:-1]]
        each = out_dev // n_space
        shift = lax.axis_index("space")
        first, rows = rows_of[-1]
        ends = placed[:, first : first + rows]
        near = []
        for offset in range(n_space):
            to = 2 * ((shift // 2 + offset // 2) % (n_space // 2)) + (shift + offset) % 2
            near.append(lax.dynamic_slice_in_dim(ends, each * to, each))
        return parts + [jnp.concatenate(near)]

    parts = lax.cond(fits, rings, direct)
    parts = parts[:-1] + [to_space(parts[-1], n_space)]
    w_scores = lax.dot_general(
        w_qk[:, :channels], w_qk[:, channels:], (((1,), (1,)), ((), ())), preferred_element_type=jnp.float32
    )
    w_scores = (w_scores * (math.log2(math.e) / math.sqrt(channels))).astype(frames.dtype)
    w_mix = jnp.dot(w_value, w_proj, preferred_element_type=jnp.float32).astype(frames.dtype)
    mixed = attend(here, parts, norm_gain[None, :], w_scores, w_mix)
    return mixed.reshape(out_dev // n_space, n_space * rows_dev, columns, channels)


def attend_kernel(n_space, sizes, here_ref, *refs):
    swapped = len(sizes) - 1
    gain_ref, score_ref, mix_ref, out_ref, normed, queries, values = refs[swapped + n_space :]
    space = here_ref[1]
    x, core = lax.shift_right_logical(space, 1), space & 1
    pieces = []
    at = 0
    for c, rows in enumerate(sizes):
        for i, offset in enumerate(far_first(n_space)):
            part = refs[c].at[i] if c < swapped else refs[swapped + i]
            down = part[...].astype(jnp.float32)
            inverse = lax.rsqrt(jnp.mean(down * down, axis=1, keepdims=True) + 1e-06)
            normed[at : at + rows, :] = (down * inverse * gain_ref[...]).astype(normed.dtype)
            source = ((x - offset // 2) & (n_space // 2 - 1)) * 2 + (core ^ (offset % 2))
            pieces.append((part, at, rows, i if c < swapped else source, sum(sizes[:c])))
            at += rows
    queries[...] = jnp.dot(normed[...], score_ref[...], preferred_element_type=jnp.float32).astype(queries.dtype)
    values[...] = jnp.dot(normed[...], mix_ref[...], preferred_element_type=jnp.float32).astype(values.dtype)
    per_block = n_space
    for b in range(0, len(pieces), per_block):
        block = pieces[b : b + per_block]
        begin, end = block[0][1], block[-1][1] + block[-1][2]
        scores = lax.dot_general(
            queries[begin:end, :], normed[...], (((1,), (1,)), ((), ())), preferred_element_type=jnp.float32
        )
        powers = jnp.exp2(scores - jnp.max(scores, axis=1, keepdims=True))
        sums = jnp.sum(powers, axis=1, keepdims=True)
        mixed = jnp.dot(powers.astype(values.dtype), values[...], preferred_element_type=jnp.float32)
        mixed = mixed / sums
        for part, at, rows, source, first in block:
            result = part[...].astype(jnp.float32) + mixed[at - begin : at - begin + rows]
            out_ref[source, first : first + rows] = result.astype(out_ref.dtype)


def attend(here, parts, norm_gain, w_scores, w_mix):
    *swapped, near = parts
    n_space = len(near)
    sizes = [part.shape[2] for part in swapped] + [near[0].shape[1]]
    frames, last, channels = near[-1].shape
    band = sum(sizes)
    total = n_space * band
    return pl.pallas_call(
        partial(attend_kernel, n_space, sizes),
        grid=(frames,),
        out_shape=jax.ShapeDtypeStruct((frames, n_space, band, channels), near[0].dtype),
        in_specs=[pl.BlockSpec(memory_space=pltpu.SMEM)]
        + [pl.BlockSpec((n_space, None, rows, channels), lambda i: (0, i, 0, 0)) for rows in sizes[:-1]]
        + [pl.BlockSpec((None, last, channels), lambda i: (i, 0, 0))] * n_space
        + [
            pl.BlockSpec((1, channels), lambda i: (0, 0)),
            pl.BlockSpec((channels, channels), lambda i: (0, 0)),
            pl.BlockSpec((channels, channels), lambda i: (0, 0)),
        ],
        out_specs=pl.BlockSpec((None, n_space, band, channels), lambda i: (i, 0, 0, 0)),
        scratch_shapes=[pltpu.VMEM((total, channels), near[0].dtype)] * 3,
        compiler_params=pltpu.CompilerParams(vmem_limit_bytes=32 * MIB),
        cost_estimate=pl.CostEstimate(
            flops=frames * total * (4 * channels * channels + 4 * total * channels),
            bytes_accessed=4 * frames * total * channels,
            transcendentals=frames * total * total,
        ),
        name="frame_attention",
    )(here, *swapped, *near, norm_gain, w_scores, w_mix)


def solution(mesh):
    placed = (P("tm", "space", None, None), P(), P(), P(), P(), P(), P(), P())
    return jax.shard_map(
        per_device,
        mesh=mesh,
        in_specs=placed,
        out_specs=P(("tm", "space"), None, None, None),
        check_vma=False,
    )
```

time: 500 us -> 147 us (0.29); the launches traced: 490 us -> 147 us
  local copies, waits for them, and re-layouts: 169 us -> 3.14 us
  waiting for transfers between devices: 196 us -> 47.1 us
  matrix products: 70.2 us -> 0.68 us
  starting transfers between devices: 29.5 us -> 61.1 us
  Pallas kernels: 15.1 us -> 34.1 us
  other arithmetic: 7.19 us -> 0.07 us
    all_to_all x3 -> x1, waiting for transfers between devices: 196 us -> 0.01 us  [swap_space(): lax.all_to_all(placed, 'space', split_axis=0, concat_axis=0, tiled=True)]
    slice x2 -> x3, local copies, waits for them, and re-layouts: 90.6 us -> 1.69 us  [the longest x1 1.01 us: per_device(): frames[fr_dev - 2:]]
    dot_general x16 -> x2, matrix products: 70.2 us -> 0.68 us  [the longest x1 0.35 us: per_device(): lax.dot_general(w_qk[:, :channels], w_qk[:, channels:], (((1,), (1,)), ((...]
    ppermute x0 -> x22, starting transfers between devices: none -> 53.4 us  [the longest x6 19.6 us: by_rings(): lax.ppermute(columns[c][dy], 'tm', ring_perm(dy))]
    ppermute x0 -> x22, waiting for transfers between devices: none -> 47.1 us  [the longest x6 15.4 us: by_rings(): lax.ppermute(merged[c][apart], both, signed_perm(n_space, apart))]
    pallas_call x0 -> x10, Pallas kernels: none -> 34.1 us  [the longest x1 13.6 us: attend(): pl.pallas_call(partial(attend_kernel, n_space, sizes), grid=(frames,), ou...]
    unnamed x19 -> x10, local copies, waits for them, and re-layouts: 32.1 us -> 0.67 us
    reshape x1, local copies, waits for them, and re-layouts: 32.1 us -> 0.76 us  [make_plan(): out_owner.reshape(-1, n_time)]
  transfers between devices with their start and end apart: 3 -> 23, of which waited for: 2 -> 12; matrix products, arithmetic and copies ran while one was open for 41% -> 1% of each run, Pallas kernels for 0% -> 9%
where the time goes in v1:
time: 147 us
  starting transfers between devices  61.1 us (42%)
  waiting for transfers between devices  47.1 us (32%)
  Pallas kernels  34.1 us (23%)
  local copies, waits for them, and re-layouts  3.14 us (2%)
    ppermute x6, starting transfers between devices, by_rings(): lax.ppermute(columns[c][dy], 'tm', ring_perm(dy))  19.6 us
    ppermute x6, waiting for transfers between devices, by_rings(): lax.ppermute(merged[c][apart], both, signed_perm(n_space, apart))  15.4 us
    ppermute x2, waiting for transfers between devices, by_rings(): lax.ppermute(far, both, signed_perm(n_space, -1))  14 us
    pallas_call x1, Pallas kernels, attend(): pl.pallas_call(partial(attend_kernel, n_space, sizes), grid=(frames,), ou...  13.6 us
    ppermute x6, waiting for transfers between devices, by_rings(): lax.ppermute(columns[c][dy], 'tm', ring_perm(dy))  12.9 us
    ppermute x6, starting transfers between devices, by_rings(): lax.ppermute(merged[c][apart], both, signed_perm(n_space, apart))  12.4 us
    ppermute x7, starting transfers between devices, to_space(): lax.ppermute(placed[each * offset:each * (offset + 1)], 'space', moves)  10.8 us
    pallas_call x2, Pallas kernels, conv(): pl.pallas_call(partial(conv_kernel, slots_row, first), grid=(1,), out_sha...  10.5 us
  transfers between devices with their start and end apart: 23, of which 12 were waited for; matrix products, arithmetic and copies ran while one was open for 1% of the time, Pallas kernels for 9%

profile of v1, /device:TPU:1, one launch (start us, length us, event | category | flops | bytes accessed | tf_op | source)
XLA Modules:
  0.0 147.3 jit_solution(1507207127761354982)
XLA Ops:
  1.0 4.4 %collective-permute-start.14 = (bf16[2,160,384]{2,1,0:T(8,128)(2,1)S(1)}, bf16[2,160,384]{2,1,0:T(8,128)(2,1)S(1)}, u32[]{:S(2)}, u32[]{:S(2)}) collective-permute-start(bf16[2,160,384]{2,1,0:T(8,128)(2,1)S(1)} %bitcast.14), channel_id=1, source_target_pairs={{0,8},{8,16},{16,24},{24,32},{32,40},{40,48},{48,56},{56,64},{64,7... | collective-permute-start | bytes 737288 | tf_op jit(solution)/shard_map/ppermute | solution.py:430
  10.0 108.0 %conditional.1 = (bf16[8,2,80,384]{3,2,1,0:T(8,128)(2,1)}, bf16[16,80,384]{2,1,0:T(8,128)(2,1)S(1)}) conditional(s32[]{:T(128)} %bitcast.5, (s32[16,128]{1,0:T(8,128)S(1)}, bf16[30,160,384]{2,1,0:T(8,128)(2,1)}, bf16[2,160,384]{2,1,0:T(8,128)(2,1)S(1)}, bf16[1152,384]{1,0:T(8,128)(2,1)}) %tuple.23, (s32[16,128]{1,0:T(8,128)S(1)}, ...), branch_computations={%region_0.1_spmd, %region_1.2_spmd} | conditional | flops 2123366400 | bytes 58344208 | solution.py:453
  10.0 6.0 %temporal_conv.4 = (bf16[16,80,384]{2,1,0:T(8,128)(2,1)S(1)}, bf16[13,80,384]{2,1,0:T(8,128)(2,1)S(1)}) custom-call(s32[16,128]{1,0:T(8,128)S(1)} %get-tuple-element.25.plan_ref, bf16[30,160,384]{2,1,0:T(8,128)(2,1)} %get-tuple-element.26.frames_ref, bf16[2,160,384]{2,1,0:T(8,128)(2,1)S(1)} %get-tuple-element.27.halo_ref, ...), custom_call_target="tpu_custom_call" | custom-call | flops 1061683200 | bytes 7249920 | tf_op jit(solution)/shard_map/cond/branch_1_fun/temporal_conv/pallas_call | solution.py:80
  16.0 6.2 %collective-permute-start = (bf16[13,80,384]{2,1,0:T(8,128)(2,1)S(1)}, bf16[13,80,384]{2,1,0:T(8,128)(2,1)S(1)}, u32[]{:S(2)}, u32[]{:S(2)}) collective-permute-start(bf16[13,80,384]{2,1,0:T(8,128)(2,1)S(1)} %get-tuple-element.30), channel_id=1, source_target_pairs={{0,8},{1,57},{2,10},{3,59},{4,12},{5,61},{6,14},{7,63},{8,0},{9,17... | collective-permute-start | bytes 2396168 | tf_op jit(solution)/shard_map/cond/branch_1_fun/ppermute | solution.py:386
  22.3 4.4 %temporal_conv.5 = (bf16[16,80,384]{2,1,0:T(8,128)(2,1)S(1)}, bf16[13,80,384]{2,1,0:T(8,128)(2,1)S(1)}) custom-call(s32[16,128]{1,0:T(8,128)S(1)} %get-tuple-element.25.plan_ref, bf16[30,160,384]{2,1,0:T(8,128)(2,1)S(1)} %copy-done.3, bf16[2,160,384]{2,1,0:T(8,128)(2,1)S(1)} %get-tuple-element.27.halo_ref, bf16[1152,384]{1,0:T(8,128)(2,1)S(1)} %copy-done.4), custom_call_target="tpu_custom_call" | custom-call | flops 1061683200 | bytes 7249920 | tf_op jit(solution)/shard_map/cond/branch_1_fun/temporal_conv/pallas_call | solution.py:80
  26.8 4.9 %collective-permute-done.refs_1_ = bf16[13,80,384]{2,1,0:T(8,128)(2,1)S(1)} collective-permute-done((bf16[13,80,384]{2,1,0:T(8,128)(2,1)S(1)}, bf16[13,80,384]{2,1,0:T(8,128)(2,1)S(1)}, u32[]{:S(2)}, u32[]{:S(2)}) %collective-permute-start) | collective-permute-done | bytes 798752 | tf_op jit(solution)/shard_map/cond/branch_1_fun/ppermute | solution.py:386
  33.4 2.9 %collective-permute-start.1 = (bf16[6,80,384]{2,1,0:T(8,128)(2,1)S(1)}, bf16[6,80,384]{2,1,0:T(8,128)(2,1)S(1)}, u32[]{:S(2)}, u32[]{:S(2)}) collective-permute-start(bf16[6,80,384]{2,1,0:T(8,128)(2,1)S(1)} %get-tuple-element.32), channel_id=1, source_target_pairs={{0,40},{1,25},{2,42},{3,27},{4,44},{5,29},{6,46},{7,31},{8,32},{9,... | collective-permute-start | bytes 1105928 | tf_op jit(solution)/shard_map/cond/branch_1_fun/ppermute | solution.py:400
  37.3 2.9 %collective-permute-start.3 = (bf16[6,80,384]{2,1,0:T(8,128)(2,1)S(1)}, bf16[6,80,384]{2,1,0:T(8,128)(2,1)S(1)}, u32[]{:S(2)}, u32[]{:S(2)}) collective-permute-start(bf16[6,80,384]{2,1,0:T(8,128)(2,1)S(1)} %get-tuple-element.34), channel_id=1, source_target_pairs={{0,56},{1,9},{2,58},{3,11},{4,60},{5,13},{6,62},{7,15},{8,16},{9,1... | collective-permute-start | bytes 1105928 | tf_op jit(solution)/shard_map/cond/branch_1_fun/ppermute | solution.py:400
  40.1 9.1 %collective-permute-done.4.refs_1_ = bf16[13,80,384]{2,1,0:T(8,128)(2,1)S(1)} collective-permute-done((bf16[13,80,384]{2,1,0:T(8,128)(2,1)S(1)}, bf16[13,80,384]{2,1,0:T(8,128)(2,1)S(1)}, u32[]{:S(2)}, u32[]{:S(2)}) %collective-permute-start.4) | collective-permute-done | bytes 798752 | tf_op jit(solution)/shard_map/cond/branch_1_fun/ppermute | solution.py:386
  50.8 4.5 %collective-permute-start.8 = (bf16[6,80,384]{2,1,0:T(8,128)(2,1)S(1)}, bf16[6,80,384]{2,1,0:T(8,128)(2,1)S(1)}, u32[]{:S(2)}, u32[]{:S(2)}) collective-permute-start(bf16[6,80,384]{2,1,0:T(8,128)(2,1)S(1)} %get-tuple-element.42), channel_id=1, source_target_pairs={{0,40},{1,25},{2,42},{3,27},{4,44},{5,29},{6,46},{7,31},{8,32},{9,... | collective-permute-start | bytes 1105928 | tf_op jit(solution)/shard_map/cond/branch_1_fun/ppermute | solution.py:400
  56.4 7.0 %collective-permute-done.2.refs_2_ = bf16[6,80,384]{2,1,0:T(8,128)(2,1)S(1)} collective-permute-done((bf16[6,80,384]{2,1,0:T(8,128)(2,1)S(1)}, bf16[6,80,384]{2,1,0:T(8,128)(2,1)S(1)}, u32[]{:S(2)}, u32[]{:S(2)}) %collective-permute-start.2) | collective-permute-done | bytes 368672 | tf_op jit(solution)/shard_map/cond/branch_1_fun/ppermute | solution.py:400
  64.8 10.0 %collective-permute-start.5 = (bf16[5,80,384]{2,1,0:T(8,128)(2,1)S(1)}, bf16[5,80,384]{2,1,0:T(8,128)(2,1)S(1)}, u32[]{:S(2)}, u32[]{:S(2)}) collective-permute-start(bf16[5,80,384]{2,1,0:T(8,128)(2,1)S(1)} %get-tuple-element.39), channel_id=1, source_target_pairs={{0,128},{8,136},{16,144},{24,152},{32,160},{40,168},{48,176},{56,1... | collective-permute-start | bytes 921608 | tf_op jit(solution)/shard_map/cond/branch_1_fun/ppermute | solution.py:411
  75.5 2.0 %collective-permute-start.7 = (bf16[5,80,384]{2,1,0:T(8,128)(2,1)S(1)}, bf16[5,80,384]{2,1,0:T(8,128)(2,1)S(1)}, u32[]{:S(2)}, u32[]{:S(2)}) collective-permute-start(bf16[5,80,384]{2,1,0:T(8,128)(2,1)S(1)} %get-tuple-element.41), channel_id=1, source_target_pairs={{0,192},{8,200},{16,208},{24,216},{32,224},{40,232},{48,240},{56,2... | collective-permute-start | bytes 921608 | tf_op jit(solution)/shard_map/cond/branch_1_fun/ppermute | solution.py:411
  77.5 6.5 %collective-permute-done.9.refs_2_ = bf16[6,80,384]{2,1,0:T(8,128)(2,1)S(1)} collective-permute-done((bf16[6,80,384]{2,1,0:T(8,128)(2,1)S(1)}, bf16[6,80,384]{2,1,0:T(8,128)(2,1)S(1)}, u32[]{:S(2)}, u32[]{:S(2)}) %collective-permute-start.9) | collective-permute-done | bytes 368672 | tf_op jit(solution)/shard_map/cond/branch_1_fun/ppermute | solution.py:400
  84.0 1.9 %collective-permute-done.10.refs_3_ = bf16[6,80,384]{2,1,0:T(8,128)(2,1)S(1)} collective-permute-done((bf16[6,80,384]{2,1,0:T(8,128)(2,1)S(1)}, bf16[6,80,384]{2,1,0:T(8,128)(2,1)S(1)}, u32[]{:S(2)}, u32[]{:S(2)}) %collective-permute-start.10) | collective-permute-done | bytes 368672 | tf_op jit(solution)/shard_map/cond/branch_1_fun/ppermute | solution.py:400
  90.6 7.6 %all-to-all-start = ((bf16[8,2,80,384]{3,2,1,0:T(8,128)(2,1)}), bf16[8,2,80,384]{3,2,1,0:T(8,128)(2,1)}, u32[]{:S(2)}, u32[]{:S(2)}) async-start(bf16[8,2,80,384]{3,2,1,0:T(8,128)(2,1)} %bitcast.1), calls=%async_computation | async-start | bytes 1966080 | tf_op jit(solution)/shard_map/cond/branch_1_fun/all_to_all | solution.py:365
  98.2 4.2 %collective-permute-start.11 = (bf16[5,80,384]{2,1,0:T(8,128)(2,1)S(1)}, bf16[5,80,384]{2,1,0:T(8,128)(2,1)S(1)}, u32[]{:S(2)}, u32[]{:S(2)}) collective-permute-start(bf16[5,80,384]{2,1,0:T(8,128)(2,1)S(1)} %get-tuple-element.46), channel_id=1, source_target_pairs={{0,128},{8,136},{16,144},{24,152},{32,160},{40,168},{48,176},{56,1... | collective-permute-start | bytes 921608 | tf_op jit(solution)/shard_map/cond/branch_1_fun/ppermute | solution.py:411
  102.8 2.3 %collective-permute-start.13 = (bf16[5,80,384]{2,1,0:T(8,128)(2,1)S(1)}, bf16[5,80,384]{2,1,0:T(8,128)(2,1)S(1)}, u32[]{:S(2)}, u32[]{:S(2)}) collective-permute-start(bf16[5,80,384]{2,1,0:T(8,128)(2,1)S(1)} %get-tuple-element.48), channel_id=1, source_target_pairs={{0,192},{8,200},{16,208},{24,216},{32,224},{40,232},{48,240},{56,2... | collective-permute-start | bytes 921608 | tf_op jit(solution)/shard_map/cond/branch_1_fun/ppermute | solution.py:411
  105.1 4.9 %collective-permute-done.11.refs_1_ = bf16[5,80,384]{2,1,0:T(8,128)(2,1)S(1)} collective-permute-done((bf16[5,80,384]{2,1,0:T(8,128)(2,1)S(1)}, bf16[5,80,384]{2,1,0:T(8,128)(2,1)S(1)}, u32[]{:S(2)}, u32[]{:S(2)}) %collective-permute-start.11) | collective-permute-done | bytes 307232 | tf_op jit(solution)/shard_map/cond/branch_1_fun/ppermute | solution.py:411
  110.0 6.7 %collective-permute-done.12.refs_2_ = bf16[5,80,384]{2,1,0:T(8,128)(2,1)S(1)} collective-permute-done((bf16[5,80,384]{2,1,0:T(8,128)(2,1)S(1)}, bf16[5,80,384]{2,1,0:T(8,128)(2,1)S(1)}, u32[]{:S(2)}, u32[]{:S(2)}) %collective-permute-start.12) | collective-permute-done | bytes 307232 | tf_op jit(solution)/shard_map/cond/branch_1_fun/ppermute | solution.py:411
  118.1 2.9 %collective-permute-start.15 = (bf16[2,80,384]{2,1,0:T(8,128)(2,1)S(1)}, bf16[2,80,384]{2,1,0:T(8,128)(2,1)S(1)}, u32[]{:S(2)}, u32[]{:S(2)}) collective-permute-start(bf16[2,80,384]{2,1,0:T(8,128)(2,1)S(1)} %get-tuple-element.61), channel_id=1, source_target_pairs={{0,4},{1,5},{2,6},{3,7},{4,0},{5,1},{6,2},{7,3},{8,12},{9,13},{10,... | collective-permute-start | bytes 368648 | tf_op jit(solution)/shard_map/ppermute | solution.py:379
  126.2 2.2 %collective-permute-start.20 = (bf16[2,80,384]{2,1,0:T(8,128)(2,1)S(1)}, bf16[2,80,384]{2,1,0:T(8,128)(2,1)S(1)}, u32[]{:S(2)}, u32[]{:S(2)}) collective-permute-start(bf16[2,80,384]{2,1,0:T(8,128)(2,1)S(1)} %get-tuple-element.56), channel_id=1, source_target_pairs={{0,7},{1,6},{2,1},{3,0},{4,3},{5,2},{6,5},{7,4},{8,15},{9,14},{10,... | collective-permute-start | bytes 368648 | tf_op jit(solution)/shard_map/ppermute | solution.py:379
  131.0 2.6 %collective-permute-done.18.refs_5_ = bf16[2,80,384]{2,1,0:T(8,128)(2,1)S(1)} collective-permute-done((bf16[2,80,384]{2,1,0:T(8,128)(2,1)S(1)}, bf16[2,80,384]{2,1,0:T(8,128)(2,1)S(1)}, u32[]{:S(2)}, u32[]{:S(2)}) %collective-permute-start.18) | collective-permute-done | bytes 122912 | tf_op jit(solution)/shard_map/ppermute | solution.py:379
  133.7 13.6 %frame_attention.1 = bf16[2,8,160,384]{3,2,1,0:T(8,128)(2,1)} custom-call(s32[2]{0:T(128)S(1)} %pad_add_fusion.place_ref.here_ref, bf16[8,2,80,384]{3,2,1,0:T(8,128)(2,1)} %get-tuple-element.51.refs_0_, bf16[16,80,384]{2,1,0:T(8,128)(2,1)S(1)} %get-tuple-element.52.refs_1_, bf16[2,80,384]{2,1,0:T(8,128)(2,1)S(1)} %collective-permute-done.15.refs_2_, ...), custom_call_target="tpu_custom_call" | custom-call | flops 6543114240 | bytes 3932160 | tf_op jit(solution)/shard_map/frame_attention/pallas_call | solution.py:505
  (55 shorter events, 26.4 us)
Async XLA Ops:
  0.0 129.3 %copy-start = (bf16[384,384]{1,0:T(8,128)(2,1)S(1)}, bf16[384,384]{1,0:T(8,128)(2,1)}, u32[]{:S(2)}) copy-start(bf16[384,384]{1,0:T(8,128)(2,1)} %param.16) | copy-start | bytes 884740
  1.0 9.0 %collective-permute-start.14 = (bf16[2,160,384]{2,1,0:T(8,128)(2,1)S(1)}, bf16[2,160,384]{2,1,0:T(8,128)(2,1)S(1)}, u32[]{:S(2)}, u32[]{:S(2)}) collective-permute-start(bf16[2,160,384]{2,1,0:T(8,128)(2,1)S(1)} %bitcast.14), channel_id=1, source_target_pairs={{0,8},{8,16},{16,24},{24,32},{32,40},{40,48},{48,56},{56,64},{64,7... | collective-permute-start | bytes 737288 | tf_op jit(solution)/shard_map/ppermute | solution.py:430
  16.0 15.7 %collective-permute-start = (bf16[13,80,384]{2,1,0:T(8,128)(2,1)S(1)}, bf16[13,80,384]{2,1,0:T(8,128)(2,1)S(1)}, u32[]{:S(2)}, u32[]{:S(2)}) collective-permute-start(bf16[13,80,384]{2,1,0:T(8,128)(2,1)S(1)} %get-tuple-element.30), channel_id=1, source_target_pairs={{0,8},{1,57},{2,10},{3,59},{4,12},{5,61},{6,14},{7,63},{8,0},{9,17... | collective-permute-start | bytes 2396168 | tf_op jit(solution)/shard_map/cond/branch_1_fun/ppermute | solution.py:386
  26.7 22.5 %collective-permute-start.4 = (bf16[13,80,384]{2,1,0:T(8,128)(2,1)S(1)}, bf16[13,80,384]{2,1,0:T(8,128)(2,1)S(1)}, u32[]{:S(2)}, u32[]{:S(2)}) collective-permute-start(bf16[13,80,384]{2,1,0:T(8,128)(2,1)S(1)} %get-tuple-element.36), channel_id=1, source_target_pairs={{0,8},{1,57},{2,10},{3,59},{4,12},{5,61},{6,14},{7,63},{8,0},{9,17... | collective-permute-start | bytes 2396168 | tf_op jit(solution)/shard_map/cond/branch_1_fun/ppermute | solution.py:386
  33.4 21.9 %collective-permute-start.1 = (bf16[6,80,384]{2,1,0:T(8,128)(2,1)S(1)}, bf16[6,80,384]{2,1,0:T(8,128)(2,1)S(1)}, u32[]{:S(2)}, u32[]{:S(2)}) collective-permute-start(bf16[6,80,384]{2,1,0:T(8,128)(2,1)S(1)} %get-tuple-element.32), channel_id=1, source_target_pairs={{0,40},{1,25},{2,42},{3,27},{4,44},{5,29},{6,46},{7,31},{8,32},{9,... | collective-permute-start | bytes 1105928 | tf_op jit(solution)/shard_map/cond/branch_1_fun/ppermute | solution.py:400
  36.3 27.1 %collective-permute-start.2 = (bf16[6,80,384]{2,1,0:T(8,128)(2,1)S(1)}, bf16[6,80,384]{2,1,0:T(8,128)(2,1)S(1)}, u32[]{:S(2)}, u32[]{:S(2)}) collective-permute-start(bf16[6,80,384]{2,1,0:T(8,128)(2,1)S(1)} %get-tuple-element.33), channel_id=1, source_target_pairs={{0,48},{1,17},{2,50},{3,19},{4,52},{5,21},{6,54},{7,23},{8,24},{9,... | collective-permute-start | bytes 1105928 | tf_op jit(solution)/shard_map/cond/branch_1_fun/ppermute | solution.py:400
  37.3 26.1 %collective-permute-start.3 = (bf16[6,80,384]{2,1,0:T(8,128)(2,1)S(1)}, bf16[6,80,384]{2,1,0:T(8,128)(2,1)S(1)}, u32[]{:S(2)}, u32[]{:S(2)}) collective-permute-start(bf16[6,80,384]{2,1,0:T(8,128)(2,1)S(1)} %get-tuple-element.34), channel_id=1, source_target_pairs={{0,56},{1,9},{2,58},{3,11},{4,60},{5,13},{6,62},{7,15},{8,16},{9,1... | collective-permute-start | bytes 1105928 | tf_op jit(solution)/shard_map/cond/branch_1_fun/ppermute | solution.py:400
  50.8 24.8 %collective-permute-start.8 = (bf16[6,80,384]{2,1,0:T(8,128)(2,1)S(1)}, bf16[6,80,384]{2,1,0:T(8,128)(2,1)S(1)}, u32[]{:S(2)}, u32[]{:S(2)}) collective-permute-start(bf16[6,80,384]{2,1,0:T(8,128)(2,1)S(1)} %get-tuple-element.42), channel_id=1, source_target_pairs={{0,40},{1,25},{2,42},{3,27},{4,44},{5,29},{6,46},{7,31},{8,32},{9,... | collective-permute-start | bytes 1105928 | tf_op jit(solution)/shard_map/cond/branch_1_fun/ppermute | solution.py:400
  55.3 28.7 %collective-permute-start.9 = (bf16[6,80,384]{2,1,0:T(8,128)(2,1)S(1)}, bf16[6,80,384]{2,1,0:T(8,128)(2,1)S(1)}, u32[]{:S(2)}, u32[]{:S(2)}) collective-permute-start(bf16[6,80,384]{2,1,0:T(8,128)(2,1)S(1)} %get-tuple-element.43), channel_id=1, source_target_pairs={{0,48},{1,17},{2,50},{3,19},{4,52},{5,21},{6,54},{7,23},{8,24},{9,... | collective-permute-start | bytes 1105928 | tf_op jit(solution)/shard_map/cond/branch_1_fun/ppermute | solution.py:400
  55.3 30.7 %collective-permute-start.10 = (bf16[6,80,384]{2,1,0:T(8,128)(2,1)S(1)}, bf16[6,80,384]{2,1,0:T(8,128)(2,1)S(1)}, u32[]{:S(2)}, u32[]{:S(2)}) collective-permute-start(bf16[6,80,384]{2,1,0:T(8,128)(2,1)S(1)} %get-tuple-element.44), channel_id=1, source_target_pairs={{0,56},{1,9},{2,58},{3,11},{4,60},{5,13},{6,62},{7,15},{8,16},{9,1... | collective-permute-start | bytes 1105928 | tf_op jit(solution)/shard_map/cond/branch_1_fun/ppermute | solution.py:400
  64.8 22.6 %collective-permute-start.5 = (bf16[5,80,384]{2,1,0:T(8,128)(2,1)S(1)}, bf16[5,80,384]{2,1,0:T(8,128)(2,1)S(1)}, u32[]{:S(2)}, u32[]{:S(2)}) collective-permute-start(bf16[5,80,384]{2,1,0:T(8,128)(2,1)S(1)} %get-tuple-element.39), channel_id=1, source_target_pairs={{0,128},{8,136},{16,144},{24,152},{32,160},{40,168},{48,176},{56,1... | collective-permute-start | bytes 921608 | tf_op jit(solution)/shard_map/cond/branch_1_fun/ppermute | solution.py:411
  74.8 13.8 %collective-permute-start.6 = (bf16[5,80,384]{2,1,0:T(8,128)(2,1)S(1)}, bf16[5,80,384]{2,1,0:T(8,128)(2,1)S(1)}, u32[]{:S(2)}, u32[]{:S(2)}) collective-permute-start(bf16[5,80,384]{2,1,0:T(8,128)(2,1)S(1)} %get-tuple-element.40), channel_id=1, source_target_pairs={{0,64},{8,72},{16,80},{24,88},{32,96},{40,104},{48,112},{56,120},{... | collective-permute-start | bytes 921608 | tf_op jit(solution)/shard_map/cond/branch_1_fun/ppermute | solution.py:411
  75.5 13.1 %collective-permute-start.7 = (bf16[5,80,384]{2,1,0:T(8,128)(2,1)S(1)}, bf16[5,80,384]{2,1,0:T(8,128)(2,1)S(1)}, u32[]{:S(2)}, u32[]{:S(2)}) collective-permute-start(bf16[5,80,384]{2,1,0:T(8,128)(2,1)S(1)} %get-tuple-element.41), channel_id=1, source_target_pairs={{0,192},{8,200},{16,208},{24,216},{32,224},{40,232},{48,240},{56,2... | collective-permute-start | bytes 921608 | tf_op jit(solution)/shard_map/cond/branch_1_fun/ppermute | solution.py:411
  90.6 27.2 %all-to-all-start = ((bf16[8,2,80,384]{3,2,1,0:T(8,128)(2,1)}), bf16[8,2,80,384]{3,2,1,0:T(8,128)(2,1)}, u32[]{:S(2)}, u32[]{:S(2)}) async-start(bf16[8,2,80,384]{3,2,1,0:T(8,128)(2,1)} %bitcast.1), calls=%async_computation | async-start | bytes 1966080 | tf_op jit(solution)/shard_map/cond/branch_1_fun/all_to_all | solution.py:365
  98.2 11.8 %collective-permute-start.11 = (bf16[5,80,384]{2,1,0:T(8,128)(2,1)S(1)}, bf16[5,80,384]{2,1,0:T(8,128)(2,1)S(1)}, u32[]{:S(2)}, u32[]{:S(2)}) collective-permute-start(bf16[5,80,384]{2,1,0:T(8,128)(2,1)S(1)} %get-tuple-element.46), channel_id=1, source_target_pairs={{0,128},{8,136},{16,144},{24,152},{32,160},{40,168},{48,176},{56,1... | collective-permute-start | bytes 921608 | tf_op jit(solution)/shard_map/cond/branch_1_fun/ppermute | solution.py:411
  102.4 14.3 %collective-permute-start.12 = (bf16[5,80,384]{2,1,0:T(8,128)(2,1)S(1)}, bf16[5,80,384]{2,1,0:T(8,128)(2,1)S(1)}, u32[]{:S(2)}, u32[]{:S(2)}) collective-permute-start(bf16[5,80,384]{2,1,0:T(8,128)(2,1)S(1)} %get-tuple-element.47), channel_id=1, source_target_pairs={{0,64},{8,72},{16,80},{24,88},{32,96},{40,104},{48,112},{56,120},{... | collective-permute-start | bytes 921608 | tf_op jit(solution)/shard_map/cond/branch_1_fun/ppermute | solution.py:411
  102.8 14.0 %collective-permute-start.13 = (bf16[5,80,384]{2,1,0:T(8,128)(2,1)S(1)}, bf16[5,80,384]{2,1,0:T(8,128)(2,1)S(1)}, u32[]{:S(2)}, u32[]{:S(2)}) collective-permute-start(bf16[5,80,384]{2,1,0:T(8,128)(2,1)S(1)} %get-tuple-element.48), channel_id=1, source_target_pairs={{0,192},{8,200},{16,208},{24,216},{32,224},{40,232},{48,240},{56,2... | collective-permute-start | bytes 921608 | tf_op jit(solution)/shard_map/cond/branch_1_fun/ppermute | solution.py:411
  118.1 8.0 %collective-permute-start.15 = (bf16[2,80,384]{2,1,0:T(8,128)(2,1)S(1)}, bf16[2,80,384]{2,1,0:T(8,128)(2,1)S(1)}, u32[]{:S(2)}, u32[]{:S(2)}) collective-permute-start(bf16[2,80,384]{2,1,0:T(8,128)(2,1)S(1)} %get-tuple-element.61), channel_id=1, source_target_pairs={{0,4},{1,5},{2,6},{3,7},{4,0},{5,1},{6,2},{7,3},{8,12},{9,13},{10,... | collective-permute-start | bytes 368648 | tf_op jit(solution)/shard_map/ppermute | solution.py:379
  121.0 7.3 %collective-permute-start.16 = (bf16[2,80,384]{2,1,0:T(8,128)(2,1)S(1)}, bf16[2,80,384]{2,1,0:T(8,128)(2,1)S(1)}, u32[]{:S(2)}, u32[]{:S(2)}) collective-permute-start(bf16[2,80,384]{2,1,0:T(8,128)(2,1)S(1)} %get-tuple-element.60), channel_id=1, source_target_pairs={{0,5},{1,4},{2,7},{3,6},{4,1},{5,0},{6,3},{7,2},{8,13},{9,12},{10,... | collective-permute-start | bytes 368648 | tf_op jit(solution)/shard_map/ppermute | solution.py:379
  122.6 8.5 %collective-permute-start.17 = (bf16[2,80,384]{2,1,0:T(8,128)(2,1)S(1)}, bf16[2,80,384]{2,1,0:T(8,128)(2,1)S(1)}, u32[]{:S(2)}, u32[]{:S(2)}) collective-permute-start(bf16[2,80,384]{2,1,0:T(8,128)(2,1)S(1)} %get-tuple-element.59), channel_id=1, source_target_pairs={{0,2},{1,3},{2,4},{3,5},{4,6},{5,7},{6,0},{7,1},{8,10},{9,11},{10,... | collective-permute-start | bytes 368648 | tf_op jit(solution)/shard_map/ppermute | solution.py:379
  124.0 9.7 %collective-permute-start.18 = (bf16[2,80,384]{2,1,0:T(8,128)(2,1)S(1)}, bf16[2,80,384]{2,1,0:T(8,128)(2,1)S(1)}, u32[]{:S(2)}, u32[]{:S(2)}) collective-permute-start(bf16[2,80,384]{2,1,0:T(8,128)(2,1)S(1)} %get-tuple-element.58), channel_id=1, source_target_pairs={{0,3},{1,2},{2,5},{3,4},{4,7},{5,6},{6,1},{7,0},{8,11},{9,10},{10,... | collective-permute-start | bytes 368648 | tf_op jit(solution)/shard_map/ppermute | solution.py:379
  124.7 9.0 %collective-permute-start.19 = (bf16[2,80,384]{2,1,0:T(8,128)(2,1)S(1)}, bf16[2,80,384]{2,1,0:T(8,128)(2,1)S(1)}, u32[]{:S(2)}, u32[]{:S(2)}) collective-permute-start(bf16[2,80,384]{2,1,0:T(8,128)(2,1)S(1)} %get-tuple-element.57), channel_id=1, source_target_pairs={{0,6},{1,7},{2,0},{3,1},{4,2},{5,3},{6,4},{7,5},{8,14},{9,15},{10,... | collective-permute-start | bytes 368648 | tf_op jit(solution)/shard_map/ppermute | solution.py:379
  126.2 7.5 %collective-permute-start.20 = (bf16[2,80,384]{2,1,0:T(8,128)(2,1)S(1)}, bf16[2,80,384]{2,1,0:T(8,128)(2,1)S(1)}, u32[]{:S(2)}, u32[]{:S(2)}) collective-permute-start(bf16[2,80,384]{2,1,0:T(8,128)(2,1)S(1)} %get-tuple-element.56), channel_id=1, source_target_pairs={{0,7},{1,6},{2,1},{3,0},{4,3},{5,2},{6,5},{7,4},{8,15},{9,14},{10,... | collective-permute-start | bytes 368648 | tf_op jit(solution)/shard_map/ppermute | solution.py:379
  128.4 5.3 %collective-permute-start.21 = (bf16[2,80,384]{2,1,0:T(8,128)(2,1)S(1)}, bf16[2,80,384]{2,1,0:T(8,128)(2,1)S(1)}, u32[]{:S(2)}, u32[]{:S(2)}) collective-permute-start(bf16[2,80,384]{2,1,0:T(8,128)(2,1)S(1)} %get-tuple-element.55), channel_id=1, source_target_pairs={{0,1},{1,0},{2,3},{3,2},{4,5},{5,4},{6,7},{7,6},{8,9},{9,8},{10,11... | collective-permute-start | bytes 368648 | tf_op jit(solution)/shard_map/ppermute | solution.py:379
  (6 other events, 268.3 us)
